TPU v7x, 128 devices: a whole 4x4x4 slice. The times are simulated.
128 devices in a mesh: row: 8 (over y, core), col: 16 (over x, z).
Axes of the slice: x: 4, y: 4, z: 4, core: 2. Of those that a mesh axis runs over, the one named last changes fastest.
Arguments:
- panel: float32 [8192, 512], P('row'), may hold values from -32 to 32, as said below
- trailing: float32 [8192, 8192], P('row', 'col'), may hold values from -86 to 86
Outputs:
- trailing_new: float32 [8192, 8192], P('row', 'col')
- reflectors: float32 [8192, 512], P('row')
Inputs may be any that keep to these rules, and one draw needn't show every extreme that they name: The diagonal entries of the panel's top 512 rows are positive and dominate the other entries of their columns in that block.
All inputs are finite; a program needn't handle non-finite values.
Results may differ from a plain program's by a relative error of at most 0.00014.
Values sent between devices are 32-bit elements; how exact they have to be, the bound alone decides.
A program may use at most 128 MiB of HBM per device.

v0:
```python
import functools
import jax, jax.numpy as jnp
from jax import lax
from jax.experimental import pallas as pl
from jax.experimental.pallas import tpu as pltpu
from jax.sharding import PartitionSpec as P

HI = lax.Precision.HIGHEST
MESH = pl.DeviceIdType.MESH
B = 64
NB = 512
NPH = NB // B
T = 128
PAIRS = [(i, j) for i in range(NB // T) for j in range(i, NB // T)]
PIECE = len(PAIRS) * T // 8


def dot(a, b):
    return lax.dot_general(a, b, (((1,), (0,)), ((), ())), precision=HI, preferred_element_type=jnp.float32)


def dot_t(a, b):
    return lax.dot_general(a, b, (((0,), (0,)), ((), ())), precision=HI, preferred_element_type=jnp.float32)


def split(a):
    hi = a.astype(jnp.bfloat16)
    return hi, (a - hi.astype(jnp.float32)).astype(jnp.bfloat16)


def dot3(a, b, dims=((1,), (0,))):
    (ah, al), (bh, bl) = (v if isinstance(v, tuple) else split(v) for v in (a, b))

    def one(p, q):
        return lax.dot_general(p, q, (dims, ((), ())), preferred_element_type=jnp.float32)

    return one(ah, bh) + (one(ah, bl) + one(al, bh))


NT = ((1,), (1,))
TN = ((0,), (0,))


def eliminate(e_ref, count):
    sub = lax.broadcasted_iota(jnp.int32, (8, 128), 0)
    rows = [[e_ref[t, 8 * i : 8 * i + 8, :] for i in range(B // 8)] for t in range(count)]

    def lane(v, k):
        return jnp.broadcast_to(v[:, k : k + 1], (8, 128))

    def row(v, k):
        return jnp.broadcast_to(v[k : k + 1, :], (8, 128))

    for jb in range(B // 8):
        full = [rows[t][jb] for t in range(count)]
        cols = [[lane(full[t], 8 * jb + m) for m in range(8)] for t in range(count)]
        kept = list(full)
        for m in range(8):
            for t in range(count):
                here = sub == m
                col = cols[t][m]
                rp = 1.0 / row(col, m)
                if m:
                    kept[t] = jnp.where(here, full[t], kept[t])
                scaled = row(full[t], m) * rp
                full[t] = jnp.where(here, scaled, full[t] - col * scaled)
                for k in range(m + 1, 8):
                    scaled = row(cols[t][k], m) * rp
                    cols[t][k] = jnp.where(here, scaled, cols[t][k] - col * scaled)
        for t in range(count):
            rows[t][jb] = kept[t]
            spread = [row(full[t], m) for m in range(8)]
            for i in range(jb + 1, B // 8):
                terms = [lane(rows[t][i], 8 * jb + m) * spread[m] for m in range(8)]
                while len(terms) > 1:
                    terms = [terms[k] + terms[k + 1] for k in range(0, len(terms), 2)]
                rows[t][i] = rows[t][i] - terms[0]
    for t in range(count):
        for i in range(B // 8):
            e_ref[t, 8 * i : 8 * i + 8, :] = rows[t][i]


def remote(src, dst, sends, recvs, n, device):
    return pltpu.make_async_remote_copy(
        src_ref=src, dst_ref=dst, send_sem=sends.at[n], recv_sem=recvs.at[n],
        device_id=device, device_id_type=MESH,
    )


class Sum:
    def __init__(self, bufs, sems, base, here):
        self.gp, self.other, self.half, self.parts, self.total = bufs
        self.sems, self.base, self.here = sems, base, here

    def fill(self, strip_of):
        for i in range(NB // T):
            strip = strip_of(i)
            for j in range(i, NB // T):
                n = PAIRS.index((i, j)) * T
                done = 0
                while done < T:
                    q, o = divmod(n + done, PIECE)
                    m = min(T - done, PIECE - o)
                    self.gp[q, o : o + m, :] = strip[done : done + m, (j - i) * T : (j - i + 1) * T]
                    done += m

    def first(self):
        k, mate = self.here["k"], self.here["mate"]
        return [remote(self.gp.at[pl.ds(4 * (1 - k), 4)], self.other, *self.sems, self.base, mate)]

    def add_pair(self):
        self.half[...] = self.gp[pl.ds(4 * self.here["k"], 4)] + self.other[...]

    def second(self):
        h = self.here
        return [
            remote(self.half.at[h["ys"][d]], self.parts.at[d], *self.sems, self.base + 1 + d, h["y_mates"][d])
            for d in range(3)
        ]

    def add_ring(self):
        k, y = self.here["k"], self.here["y"]
        self.total[4 * k + y] = (self.half[y] + self.parts[0]) + (self.parts[1] + self.parts[2])

    def third(self):
        h = self.here
        slot = self.total.at[4 * h["k"] + h["y"]]
        return [remote(slot, slot, *self.sems, self.base + 4 + d, h["y_mates"][d]) for d in range(3)]

    def fourth(self):
        group = self.total.at[pl.ds(4 * self.here["k"], 4)]
        return [remote(group, group, *self.sems, self.base + 7, self.here["mate"])]

    def unpack(self, store):
        for n, (i, j) in enumerate(PAIRS):
            done = 0
            while done < T:
                q, o = divmod(n * T + done, PIECE)
                m = min(T - done, PIECE - o)
                store(i * T + done, m, j * T, self.total[q, o : o + m, :])
                done += m


def start(copies):
    for cp in copies:
        cp.start()


def wait(copies):
    for cp in copies:
        cp.wait()


def step_kernel(
    panel_ref, trail_ref, out_ref, vec_ref,
    r_ref, rit_ref, lui_ref, mi_ref, x_ref, s_ref, e_ref,
    g0, g1, g2, g3, g4, c0, c1, c2, c3, c4,
    top, zp, zo, zh, zparts, zc, zs, xs, xt8, az0, az1, ax0, ax1, py, pc, qc,
    k2t, img, wr, vc, yct, cc, sends, recvs,
):
    r, c = lax.axis_index("row"), lax.axis_index("col")
    y, k = lax.div(r, 2), lax.rem(r, 2)
    x, z = lax.div(c, 4), lax.rem(c, 4)
    ys = [lax.rem(y + d, 4) for d in range(1, 4)]
    mate = (2 * y + 1 - k, c)
    y_mates = [(2 * v + k, c) for v in ys]
    y_cross = [(2 * v + 1 - k, c) for v in ys]
    x_mates = [(r, lax.rem(x + d, 4) * 4 + z) for d in range(1, 4)]
    z_mates = [(r, x * 4 + lax.rem(z + d, 4)) for d in range(1, 4)]
    peers = [mate] + y_mates + y_cross + x_mates + z_mates
    sems = (sends, recvs)
    here = {"k": k, "y": y, "ys": ys, "mate": mate, "y_mates": y_mates}
    to_r, to_c = lax.div(c, 2), 8 * lax.rem(c, 2) + r
    from_r, from_c = lax.rem(c, 8), 2 * r + lax.div(c, 8)
    fixed = (to_r == r) & (to_c == c)

    barrier = pltpu.get_barrier_semaphore()
    for peer in peers:
        pl.semaphore_signal(barrier, inc=1, device_id=peer, device_id_type=MESH)

    @pl.when(jnp.logical_not(fixed))
    def _():
        pl.semaphore_signal(barrier, inc=1, device_id=(from_r, from_c), device_id_type=MESH)

    lone = (r == 0) & (c == 0)

    @pl.when(jnp.logical_not(lone))
    def _():
        pl.semaphore_signal(barrier, inc=1, device_id=(0, 2 * r + lax.div(c, 8)), device_id_type=MESH)

    gram = Sum((g0, g1, g2, g3, g4), sems, 0, here)
    curv = Sum((c0, c1, c2, c3, c4), sems, 8, here)
    TOP, ZRS, ZAG, PERM, XSC, AXA, AXB, AZA, AZB, PAN, QQ = 16, 24, 28, 32, 33, 34, 40, 46, 52, 58, 66
    FAN = 72

    gram.fill(lambda i: dot_t(panel_ref[:, i * T : (i + 1) * T], panel_ref[:, i * T :]))

    pl.semaphore_wait(barrier, len(peers) + jnp.where(r == 0, 8, 0) - jnp.where(lone, 1, 0) + jnp.where(fixed, 0, 1))

    def top_out():
        out = []
        for n, peer in enumerate([(1, c)] + [(2 * v + q, c) for v in range(1, 4) for q in range(2)]):
            q = 1 if n == 0 else (n - 1) % 2
            place = x + 4 * z if q == 0 else z + 4 * x
            out.append(pltpu.make_async_remote_copy(
                src_ref=panel_ref.at[pl.ds(pl.multiple_of(32 * c + 16 * q, 16), 16)],
                dst_ref=top.at[q, place], send_sem=sends.at[FAN + n], recv_sem=recvs.at[TOP],
                device_id=peer, device_id_type=MESH))
        return out

    mine = jnp.where(k == 0, x + 4 * z, z + 4 * x)

    def top_spread(base, src, peers_0, peers_1):
        return [
            remote(src, src, sends, recvs, base + d, (r, jnp.where(k == 0, peers_0[d][1], peers_1[d][1])))
            for d in range(3)
        ]

    top_a = lambda: top_spread(TOP + 1, top.at[k, mine], x_mates, z_mates)
    top_b = lambda: top_spread(TOP + 4, top.at[k, pl.ds(4 * jnp.where(k == 0, z, x), 4)], z_mates, x_mates)
    top_c = lambda: [remote(top.at[k], top.at[k], sends, recvs, TOP + 7, mate)]

    def first_cols_out(n):
        return pltpu.make_async_remote_copy(
            src_ref=xt8.at[n], dst_ref=xs, send_sem=sends.at[FAN + 7 + n],
            recv_sem=recvs.at[XSC], device_id=(lax.div(c, 2), 8 * lax.rem(c, 2) + n), device_id_type=MESH)

    def first_cols(act):
        for n in range(1, 8):
            act(first_cols_out(n))

        @pl.when(c > 0)
        def _():
            act(first_cols_out(0))

    def gather_a(src, h0, h1, base):
        return [remote(src.at[pl.ds(0, 32)], h0.at[4 * z + x], sends, recvs, base + d, x_mates[d]) for d in range(3)] + [
            remote(src.at[pl.ds(32, 32)], h1.at[4 * x + z], sends, recvs, base + 3 + d, z_mates[d]) for d in range(3)]

    def gather_own(src, h0, h1):
        h0[4 * z + x] = src[0:32, :]
        h1[4 * x + z] = src[32:64, :]

    def gather_b(h0, h1, base):
        g0_, g1_ = h0.at[pl.ds(4 * z, 4)], h1.at[pl.ds(4 * x, 4)]
        return [remote(g0_, g0_, sends, recvs, base + d, z_mates[d]) for d in range(3)] + [
            remote(g1_, g1_, sends, recvs, base + 3 + d, x_mates[d]) for d in range(3)]

    def z_first():
        return [remote(zp.at[pl.ds(4 * (1 - k), 4)], zo, sends, recvs, ZRS, mate)]

    def z_second():
        return [remote(zh.at[ys[d]], zparts.at[d], sends, recvs, ZRS + 1 + d, y_mates[d]) for d in range(3)]

    def z_third():
        slot = zc.at[y, k]
        return [remote(slot, slot, sends, recvs, ZAG + d, y_mates[d]) for d in range(3)]

    def z_fourth():
        return [remote(zc.at[:, k], zc.at[:, k], sends, recvs, ZAG + 3, mate)]

    def z_move():
        return remote(zc.at[y, k], zs, sends, recvs, PERM, (to_r, to_c))

    def block_first(src_half, dst, base, at_y, at_k):
        return remote(src_half, dst.at[1 - at_k], sends, recvs, base, mate)

    def block_second(dst, base, at_y):
        return [remote(dst.at[k], dst.at[k], sends, recvs, base + 1 + d, y_mates[d]) for d in range(3)]

    def block_third(dst, base):
        return [remote(dst.at[k], dst.at[k], sends, recvs, base + 4, mate)]

    giver = k == lax.div(z, 2)
    given = 512 * lax.rem(z, 2)

    def pan_first():
        out = []
        for d in range(3):
            for q, peer in ((0, (2 * ys[d], c)), (1, (2 * ys[d] + 1, c))):
                out.append(pltpu.make_async_remote_copy(
                    src_ref=panel_ref.at[pl.ds(pl.multiple_of(given + 128 * x + 64 * q, 64), 64)],
                    dst_ref=py.at[d], send_sem=sends.at[FAN + 22 + 2 * d + q], recv_sem=recvs.at[PAN + d],
                    device_id=peer, device_id_type=MESH))
        return out

    def pan_first_arrived():
        for d in range(3):
            remote(py.at[d], py.at[d], sends, recvs, PAN + d, mate).wait_recv()

    def pan_second(act):
        for d in range(3):
            xt = lax.rem(x + d + 1, 4)

            @pl.when(xt != y)
            def _():
                act(remote(py.at[lax.rem(y - xt + 4, 4) - 1], pc.at[k, x], sends, recvs, PAN + 3 + d, (r, 4 * xt + z)))

    def pan_third(q, n):
        return remote(pc.at[q], pc.at[q], sends, recvs, PAN + 6 + n, mate)

    start(gram.first())
    pl.when(r == 0)(lambda: start(top_out()))

    @pl.when(r == 0)
    def _():
        for n in range(4):
            block = trail_ref[0:512, 128 * n : 128 * (n + 1)].T
            xt8[2 * n] = block[0:64, :]
            xt8[2 * n + 1] = block[64:128, :]
        first_cols(lambda cp: cp.start())
        block_first(trail_ref.at[pl.ds(256, 256)], qc, QQ, 0, 0).start()
        qc[0] = trail_ref[0:256, :]
        top[0, x + 4 * z] = panel_ref[pl.ds(pl.multiple_of(32 * c, 32), 16), :]

    @pl.when(lone)
    def _():
        xs[...] = xt8[0]

    wait(gram.first())
    gram.add_pair()
    start(gram.second())

    for half in range(2):
        acc = None
        for q in range(4):
            left = trail_ref[256 * q : 256 * (q + 1), 256 * half : 256 * (half + 1)].T
            term = dot3(left, panel_ref[256 * q : 256 * (q + 1), :])
            acc = term if acc is None else acc + term
        for q in range(4):
            s = 4 * half + q
            zp[4 * (s % 2) + s // 2] = acc[64 * q : 64 * (q + 1), :]
    start(z_first())

    @pl.when(r > 0)
    def _():
        remote(top.at[k, mine], top.at[k, mine], sends, recvs, TOP, mate).wait_recv()

    start(top_a())
    wait(gram.second())
    gram.add_ring()
    start(gram.third())
    wait(z_first())
    zh[...] = zp[pl.ds(4 * k, 4)] + zo[...]
    wait(top_a())
    start(top_b())
    wait(gram.third())
    start(gram.fourth())
    start(z_second())
    pl.when(giver)(lambda: start(pan_first()))
    wait(gram.fourth())

    def put(i, m, j, v):
        x_ref[i : i + m, j : j + T] = v

    gram.unpack(put)
    wait(top_b())
    start(top_c())

    @pl.when(jnp.logical_not(lone))
    def _():
        remote(xs, xs, sends, recvs, XSC, mate).wait_recv()

    gather_own(xs, ax0, ax1)
    start(gather_a(xs, ax0, ax1, AXA))

    def mid0():
        wait(z_second())
        zc[y, k] = (zh[y] + zparts[0]) + (zparts[1] + zparts[2])

        @pl.when(fixed)
        def _():
            zs[...] = zc[y, k]

        @pl.when(jnp.logical_not(fixed))
        def _():
            z_move().start()

        start(z_third())

    def hook0():
        wait(top_c())
        for a in range(4):
            for b in range(4):
                s_ref[32 * (4 * a + b) : 32 * (4 * a + b) + 16, :] += top[0, a + 4 * b]
                s_ref[32 * (4 * a + b) + 16 : 32 * (4 * a + b) + 32, :] += top[1, b + 4 * a]

    def mid1():
        wait(gather_a(xs, ax0, ax1, AXA))
        start(gather_b(ax0, ax1, AXB))

    def hook1():
        @pl.when(jnp.logical_not(fixed))
        def _():
            z_move().wait()

        gather_own(zs, az0, az1)
        start(gather_a(zs, az0, az1, AZA))

    def mid2():
        pan_first_arrived()
        pan_second(lambda cp: cp.start())

        @pl.when(x != y)
        def _():
            pc[k, x] = py[lax.rem(y - x + 4, 4) - 1]

        @pl.when((x == y) & giver)
        def _():
            for q in range(4):
                for h in range(2):
                    pc[h, q] = panel_ref[pl.ds(pl.multiple_of(given + 128 * q + 64 * h, 64), 64), :]
            pan_third(k, 0).start()
            pan_third(1 - k, 1).start()

        @pl.when(y == 0)
        def _():
            @pl.when(k != 0)
            def _():
                block_first(trail_ref.at[pl.ds(256, 256)], qc, QQ, 0, 0).wait_recv()

            start(block_second(qc, QQ, 0))

    def hook2():
        wait(z_third())
        start(z_fourth())

    def hook3():
        wait(gather_a(zs, az0, az1, AZA))
        start(gather_b(az0, az1, AZB))

    def hook4():
        @pl.when(x != y)
        def _():
            for d in range(3):
                remote(pc.at[k, 0], pc.at[k, 0], sends, recvs, PAN + 3 + d, mate).wait_recv()
            pan_third(k, 0).start()

    def block_arrive(dst, base, at_y):
        @pl.when(y == at_y)
        def _():
            for cp in block_second(dst, base, at_y):
                cp.wait_send()

        @pl.when(y != at_y)
        def _():
            for d in range(3):
                @pl.when(lax.rem(at_y + d + 1, 4) == y)
                def _():
                    block_second(dst, base, at_y)[d].wait_recv()

        start(block_third(dst, base))

    def hook6():
        wait(z_fourth())
        wait(gather_b(ax0, ax1, AXB))
        pan_second(lambda cp: cp.wait_send())

        @pl.when(x != y)
        def _():
            pan_third(k, 0).wait()

        @pl.when((x == y) & giver)
        def _():
            pan_third(k, 0).wait_send()
            pan_third(1 - k, 1).wait_send()

        @pl.when((x == y) & jnp.logical_not(giver))
        def _():
            pan_third(1 - k, 0).wait_recv()
            pan_third(k, 1).wait_recv()

    def hook7():
        block_arrive(qc, QQ, 0)

    def hook8():
        wait(block_third(qc, QQ))
        wait(gather_b(az0, az1, AZB))

        @pl.when(giver)
        def _():
            for cp in pan_first():
                cp.wait_send()

        @pl.when(r == 0)
        def _():
            for cp in top_out():
                cp.wait_send()
            first_cols(lambda cp: cp.wait_send())
            block_first(trail_ref.at[pl.ds(256, 256)], qc, QQ, 0, 0).wait_send()


    mids = {0: mid0, 1: mid1, 2: mid2}
    hooks = {0: hook0, 1: hook1, 2: hook2, 3: hook3, 4: hook4, 6: hook6, 7: hook7, 8: hook8}
    r_i = lax.broadcasted_iota(jnp.int32, (B, B), 0)
    c_i = lax.broadcasted_iota(jnp.int32, (B, B), 1)
    eye = (r_i == c_i).astype(jnp.float32)
    s_ref[...] = jnp.zeros_like(s_ref)
    r_ref[...] = jnp.zeros_like(r_ref)
    rit_ref[...] = jnp.zeros_like(rit_ref)
    lui_ref[...] = jnp.zeros_like(lui_ref)
    mi_ref[...] = jnp.zeros_like(mi_ref)
    for t in range(3):
        e_ref[t, :, :B] = eye
        e_ref[t, :, B:] = eye

    def diag(v):
        return jnp.sum(jnp.where(r_i == c_i, v, 0.0), axis=1, keepdims=True)

    def pre(p):
        a, b = p * B, (p + 1) * B
        if p < NPH:
            block = x_ref[a:b, a:b]
            e_ref[0, :, :B] = jnp.where(r_i <= c_i, block, block.T)
            e_ref[0, :, B:] = eye
        if p > 0:
            a, b = a - B, b - B
            block = s_ref[a:b, a:b]
            e_ref[1, :, :B] = block
            e_ref[1, :, B:] = eye
            e_ref[2, :, :B] = block.T
            e_ref[2, :, B:] = eye

    def post(p):
        a, b = p * B, (p + 1) * B
        if p < NPH:
            left = e_ref[0, :, :B]
            rs = lax.rsqrt(diag(left))
            linv = rs * e_ref[0, :, B:]
            rpp = jnp.where(r_i <= c_i, rs * left, 0.0)
            r_ref[a:b, a:b] = rpp
            rit_ref[a:b, a:b] = linv
            if p:
                rit_ref[a:b, :a] = dot(linv, rit_ref[a:b, :a])
            s_ref[a:b, a:b] += rpp
            if b < NB:
                rrow = dot(linv, x_ref[a:b, b:])
                r_ref[a:b, b:] = rrow
                s_ref[a:b, b:] += rrow
                x_ref[b:, b:] -= dot_t(rrow, rrow)
                rit_ref[b:, :b] -= dot_t(rrow, rit_ref[a:b, :b])
        if p > 0:
            a, b = a - B, b - B
            lui = e_ref[1, :, B:]
            mit = (1.0 / diag(e_ref[2, :, :B])) * e_ref[2, :, B:]
            mi = mit.T
            lui_ref[a:b, a:b] = lui
            mi_ref[a:b, a:b] = mi
            if a:
                lui_ref[a:b, :a] = dot(lui, lui_ref[a:b, :a])
                mi_ref[:a, a:b] = dot(mi_ref[:a, a:b], mi)
            if b < NB:
                mrow = dot(lui, s_ref[a:b, b:])
                lucol = dot(s_ref[b:, a:b], mi)
                s_ref[b:, b:] -= dot(lucol, mrow)
                lui_ref[b:, :b] -= dot(lucol, lui_ref[a:b, :b])
                mi_ref[:b, b:] -= dot(mi_ref[:b, a:b], mrow)

    def phase(ph, carry):
        for p in range(NPH + 1):
            pl.when(ph == p)(functools.partial(pre, p))
        eliminate(e_ref, 3)
        for p, hook in mids.items():
            pl.when(ph == p)(hook)
        for p in range(NPH + 1):
            pl.when(ph == p)(functools.partial(post, p))
        for p, hook in hooks.items():
            pl.when(ph == p)(hook)
        return carry

    lax.fori_loop(0, NPH + 1, phase, 0)


    k2t[...] = dot3(lui_ref[...], rit_ref[...])
    k2 = split(k2t[...])
    lui = split(lui_ref[...])
    for az, ax, h in ((az0, ax0, 0), (az1, ax1, 1)):
        val = dot3(az[...].reshape(NB, NB), k2, NT) + dot3(ax[...].reshape(NB, NB), lui, NT)
        for n in range(16):
            j = 4 * (n % 4) + n // 4 if h == 0 else n
            img[64 * j + 32 * h : 64 * j + 32 * h + 32, :] = val[32 * n : 32 * n + 32, :]

    def shifted(q):
        block = panel_ref[256 * q : 256 * (q + 1), :]
        if q < 2:
            block = block + jnp.where(r == 0, r_ref[256 * q : 256 * (q + 1), :], 0.0)
        return block

    for q in range(4):
        wr[256 * q : 256 * (q + 1), :] = dot3(shifted(q), k2, NT)
    curv.fill(lambda i: dot3(wr[:, i * T : (i + 1) * T].T, img[:, i * T :]))
    start(curv.first())
    mi = split(mi_ref[...])
    for q in range(4):
        for h in range(2):
            rows = pl.ds(128 * q + 64 * h, 64)
            vc[rows, :] = pc[h, q] + jnp.where(c == 0, r_ref[rows, :], 0.0)
    vc[...] = dot3(vc[...], mi)
    wait(curv.first())
    curv.add_pair()
    start(curv.second())
    for q in range(4):
        vec_ref[256 * q : 256 * (q + 1), :] = dot3(shifted(q), mi)
    wait(curv.second())
    curv.add_ring()
    start(curv.third())
    yct[...] = dot3(k2, zc[...].reshape(NB, NB), NT) + dot3(lui, qc[...].reshape(NB, NB))
    wait(curv.third())
    start(curv.fourth())
    vcs = split(vc[...])
    for q in range(4):
        rows = pl.ds(256 * q, 256)
        out_ref[rows, :] = trail_ref[rows, :] - dot3(img[rows, :], vcs, NT)
    wait(curv.fourth())

    def put_c(i, m, j, v):
        cc[i : i + m, j : j + T] = v
        if i // T * T != j:
            cc[j : j + T, i : i + m] = v.T

    curv.unpack(put_c)
    dct = split(yct[...] - dot3(cc[...], vcs, NT))
    for q in range(4):
        rows = pl.ds(256 * q, 256)
        out_ref[rows, :] -= dot3(vec_ref[rows, :], dct)


def on_device(panel, trailing):
    f32 = jnp.float32
    vm = pl.BlockSpec(memory_space=pltpu.VMEM)
    sq = pltpu.VMEM((NB, NB), f32)
    sums = [(8, PIECE, T), (4, PIECE, T), (4, PIECE, T), (3, PIECE, T), (8, PIECE, T)]
    shapes = [(NB, NB)] * 6 + [(3, B, 2 * B)] + sums * 2 + [
        (2, 16, 16, NB),
        (8, 64, NB), (4, 64, NB), (4, 64, NB), (3, 64, NB), (4, 2, 64, NB),
        (64, NB), (64, NB), (8, 64, NB),
        (16, 32, NB), (16, 32, NB), (16, 32, NB), (16, 32, NB),
        (3, 64, NB), (2, 4, 64, NB), (2, 256, NB),
        (NB, NB), (1024, NB), (1024, NB), (NB, NB), (NB, NB), (NB, NB),
    ]
    return tuple(pl.pallas_call(
        step_kernel,
        out_shape=[jax.ShapeDtypeStruct((1024, NB), f32)] * 2,
        in_specs=[vm] * 2,
        out_specs=[vm] * 2,
        scratch_shapes=[pltpu.VMEM(s, f32) for s in shapes]
        + [pltpu.SemaphoreType.DMA((104,)), pltpu.SemaphoreType.DMA((72,))],
        compiler_params=pltpu.CompilerParams(
            vmem_limit_bytes=56 * 1024 * 1024, collective_id=0, has_side_effects=True),
        name="step",
    )(panel, trailing))


def solution(mesh):
    return jax.shard_map(
        on_device,
        mesh=mesh,
        in_specs=(P("row", None), P("row", "col")),
        out_specs=(P("row", "col"), P("row", None)),
        check_vma=False,
    )
```

profile of v0, /device:TPU:0, one launch (start us, length us, event | category | flops | bytes accessed | tf_op | source)
XLA Modules:
  0.0 122.5 jit_solution(8806794575424159461)
XLA Ops:
  0.6 117.3 %step.1 = (f32[1024,512]{1,0:T(8,128)}, f32[1024,512]{1,0:T(8,128)}) custom-call(f32[1024,512]{1,0:T(8,128)} %panel_ref.1, f32[1024,512]{1,0:T(8,128)} %trail_ref.1), custom_call_target="tpu_custom_call" | custom-call | tf_op jit(solution)/shard_map/step/pallas_call | solution.py:641
  118.0 0.0 copy-start
  118.0 3.2 %copy.6 = f32[1024,512]{1,0:T(8,128)} copy(f32[1024,512]{1,0:T(8,128)} %get-tuple-element.4) | data formatting | bytes 4194304
  121.2 0.0 copy-done
  121.2 1.3 %copy.7 = f32[1024,512]{1,0:T(8,128)} copy(f32[1024,512]{1,0:T(8,128)S(1)} %copy-done) | data formatting | bytes 4194304
Async XLA Ops:
  118.0 3.2 %copy-start = (f32[1024,512]{1,0:T(8,128)S(1)}, f32[1024,512]{1,0:T(8,128)}, u32[]{:S(2)}) copy-start(f32[1024,512]{1,0:T(8,128)} %get-tuple-element.5) | copy-start | bytes 6291460
where the time goes:
time: 124 us; the launch traced here: 123 us
  Pallas kernels  117 us (94%)
  local copies, waits for them, and re-layouts  4.55 us (4%)
    pallas_call x1, Pallas kernels, on_device(): pl.pallas_call(step_kernel, out_shape=[jax.ShapeDtypeStruct((1024, NB), f...  117 us
    unnamed x4, local copies, waits for them, and re-layouts  4.55 us

commit v1 on v0

--- a/solution.py
+++ b/solution.py
@@ -155,7 +155,7 @@
     panel_ref, trail_ref, out_ref, vec_ref,
     r_ref, rit_ref, lui_ref, mi_ref, x_ref, s_ref, e_ref,
     g0, g1, g2, g3, g4, c0, c1, c2, c3, c4,
-    top, zp, zo, zh, zparts, zc, zs, xs, xt8, az0, az1, ax0, ax1, py, pc, qc,
+    top, zp, zo, zh, zparts, zc, zs, xs, sx0, sx1, rx0, rx1, az0, az1, ax0, ax1, py, pc, qc,
     k2t, img, wr, vc, yct, cc, sends, recvs,
 ):
     r, c = lax.axis_index("row"), lax.axis_index("col")
@@ -182,20 +182,15 @@
     def _():
         pl.semaphore_signal(barrier, inc=1, device_id=(from_r, from_c), device_id_type=MESH)
 
-    lone = (r == 0) & (c == 0)
-
-    @pl.when(jnp.logical_not(lone))
-    def _():
-        pl.semaphore_signal(barrier, inc=1, device_id=(0, 2 * r + lax.div(c, 8)), device_id_type=MESH)
 
     gram = Sum((g0, g1, g2, g3, g4), sems, 0, here)
     curv = Sum((c0, c1, c2, c3, c4), sems, 8, here)
-    TOP, ZRS, ZAG, PERM, XSC, AXA, AXB, AZA, AZB, PAN, QQ = 16, 24, 28, 32, 33, 34, 40, 46, 52, 58, 66
-    FAN = 72
+    TOP, ZRS, ZAG, PERM, XSC, AXA, AXB, AZA, AZB, PAN, QQ = 16, 24, 28, 32, 33, 37, 43, 49, 55, 61, 69
+    FAN = 76
 
     gram.fill(lambda i: dot_t(panel_ref[:, i * T : (i + 1) * T], panel_ref[:, i * T :]))
 
-    pl.semaphore_wait(barrier, len(peers) + jnp.where(r == 0, 8, 0) - jnp.where(lone, 1, 0) + jnp.where(fixed, 0, 1))
+    pl.semaphore_wait(barrier, len(peers) + jnp.where(fixed, 0, 1))
 
     def top_out():
         out = []
@@ -220,18 +215,53 @@
     top_b = lambda: top_spread(TOP + 4, top.at[k, pl.ds(4 * jnp.where(k == 0, z, x), 4)], z_mates, x_mates)
     top_c = lambda: [remote(top.at[k], top.at[k], sends, recvs, TOP + 7, mate)]
 
-    def first_cols_out(n):
-        return pltpu.make_async_remote_copy(
-            src_ref=xt8.at[n], dst_ref=xs, send_sem=sends.at[FAN + 7 + n],
-            recv_sem=recvs.at[XSC], device_id=(lax.div(c, 2), 8 * lax.rem(c, 2) + n), device_id_type=MESH)
-
-    def first_cols(act):
-        for n in range(1, 8):
-            act(first_cols_out(n))
-
-        @pl.when(c > 0)
-        def _():
-            act(first_cols_out(0))
+    def scatter_first():
+        out = []
+        for d in range(3):
+            out.append(pltpu.make_async_remote_copy(
+                src_ref=sx0.at[d + 1], dst_ref=rx0, send_sem=sends.at[FAN + 7 + d], recv_sem=recvs.at[XSC],
+                device_id=(r, d + 1), device_id_type=MESH))
+            out.append(pltpu.make_async_remote_copy(
+                src_ref=sx1.at[d + 1], dst_ref=rx1, send_sem=sends.at[FAN + 10 + d], recv_sem=recvs.at[XSC + 1],
+                device_id=(r, 4 * (d + 1)), device_id_type=MESH))
+        return out
+
+    def scatter_second(axis):
+        out = []
+        for d in range(3):
+            src, dst, to = (rx0, 0, 4 * (d + 1) + z) if axis == 0 else (rx1, 32, 4 * x + d + 1)
+            out.append(pltpu.make_async_remote_copy(
+                src_ref=src.at[d + 1], dst_ref=xs.at[pl.ds(dst, 32)], send_sem=sends.at[FAN + 13 + 3 * axis + d],
+                recv_sem=recvs.at[XSC + 2 + axis], device_id=(r, to), device_id_type=MESH))
+        return out
+
+    def scatter_relay():
+        @pl.when((x == 0) & (z > 0))
+        def _():
+            remote(rx0, rx0, sends, recvs, XSC, mate).wait_recv()
+
+        @pl.when((z == 0) & (x > 0))
+        def _():
+            remote(rx1, rx1, sends, recvs, XSC + 1, mate).wait_recv()
+
+        @pl.when(x == 0)
+        def _():
+            start(scatter_second(0))
+            xs[0:32, :] = rx0[0]
+
+        @pl.when(z == 0)
+        def _():
+            start(scatter_second(1))
+            xs[32:64, :] = rx1[0]
+
+    def scatter_arrived():
+        @pl.when(x > 0)
+        def _():
+            remote(rx0.at[0], rx0.at[0], sends, recvs, XSC + 2, mate).wait_recv()
+
+        @pl.when(z > 0)
+        def _():
+            remote(rx1.at[0], rx1.at[0], sends, recvs, XSC + 3, mate).wait_recv()
 
     def gather_a(src, h0, h1, base):
         return [remote(src.at[pl.ds(0, 32)], h0.at[4 * z + x], sends, recvs, base + d, x_mates[d]) for d in range(3)] + [
@@ -304,18 +334,18 @@
 
     @pl.when(r == 0)
     def _():
-        for n in range(4):
-            block = trail_ref[0:512, 128 * n : 128 * (n + 1)].T
-            xt8[2 * n] = block[0:64, :]
-            xt8[2 * n + 1] = block[64:128, :]
-        first_cols(lambda cp: cp.start())
         block_first(trail_ref.at[pl.ds(256, 256)], qc, QQ, 0, 0).start()
         qc[0] = trail_ref[0:256, :]
         top[0, x + 4 * z] = panel_ref[pl.ds(pl.multiple_of(32 * c, 32), 16), :]
 
-    @pl.when(lone)
+    @pl.when(c == 0)
     def _():
-        xs[...] = xt8[0]
+        for n in range(16):
+            sx0[n % 4, n // 4] = trail_ref[64 * n : 64 * n + 32, :]
+            sx1[n // 4, n % 4] = trail_ref[64 * n + 32 : 64 * n + 64, :]
+        start(scatter_first())
+        rx0[...] = sx0[0]
+        rx1[...] = sx1[0]
 
     wait(gram.first())
     gram.add_pair()
@@ -344,6 +374,7 @@
     zh[...] = zp[pl.ds(4 * k, 4)] + zo[...]
     wait(top_a())
     start(top_b())
+    scatter_relay()
     wait(gram.third())
     start(gram.fourth())
     start(z_second())
@@ -357,10 +388,7 @@
     wait(top_b())
     start(top_c())
 
-    @pl.when(jnp.logical_not(lone))
-    def _():
-        remote(xs, xs, sends, recvs, XSC, mate).wait_recv()
-
+    scatter_arrived()
     gather_own(xs, ax0, ax1)
     start(gather_a(xs, ax0, ax1, AXA))
 
@@ -486,8 +514,22 @@
         def _():
             for cp in top_out():
                 cp.wait_send()
-            first_cols(lambda cp: cp.wait_send())
             block_first(trail_ref.at[pl.ds(256, 256)], qc, QQ, 0, 0).wait_send()
+
+        @pl.when(c == 0)
+        def _():
+            for cp in scatter_first():
+                cp.wait_send()
+
+        @pl.when(x == 0)
+        def _():
+            for cp in scatter_second(0):
+                cp.wait_send()
+
+        @pl.when(z == 0)
+        def _():
+            for cp in scatter_second(1):
+                cp.wait_send()
 
 
     mids = {0: mid0, 1: mid1, 2: mid2}
@@ -633,7 +675,7 @@
     shapes = [(NB, NB)] * 6 + [(3, B, 2 * B)] + sums * 2 + [
         (2, 16, 16, NB),
         (8, 64, NB), (4, 64, NB), (4, 64, NB), (3, 64, NB), (4, 2, 64, NB),
-        (64, NB), (64, NB), (8, 64, NB),
+        (64, NB), (64, NB), (4, 4, 32, NB), (4, 4, 32, NB), (4, 32, NB), (4, 32, NB),
         (16, 32, NB), (16, 32, NB), (16, 32, NB), (16, 32, NB),
         (3, 64, NB), (2, 4, 64, NB), (2, 256, NB),
         (NB, NB), (1024, NB), (1024, NB), (NB, NB), (NB, NB), (NB, NB),
@@ -644,7 +686,7 @@
         in_specs=[vm] * 2,
         out_specs=[vm] * 2,
         scratch_shapes=[pltpu.VMEM(s, f32) for s in shapes]
-        + [pltpu.SemaphoreType.DMA((104,)), pltpu.SemaphoreType.DMA((72,))],
+        + [pltpu.SemaphoreType.DMA((108,)), pltpu.SemaphoreType.DMA((76,))],
         compiler_params=pltpu.CompilerParams(
             vmem_limit_bytes=56 * 1024 * 1024, collective_id=0, has_side_effects=True),
         name="step",

time: 124 us -> 113 us (0.911)
  Pallas kernels: 117 us -> 107 us
    pallas_call x1, Pallas kernels: 117 us -> 107 us  [on_device(): pl.pallas_call(step_kernel, out_shape=[jax.ShapeDtypeStruct((1024, NB), f...]
where the time goes in v1:
time: 113 us; the launch traced here: 112 us
  Pallas kernels  107 us (95%)
  local copies, waits for them, and re-layouts  4.55 us (4%)
    pallas_call x1, Pallas kernels, on_device(): pl.pallas_call(step_kernel, out_shape=[jax.ShapeDtypeStruct((1024, NB), f...  107 us
    unnamed x4, local copies, waits for them, and re-layouts  4.55 us

profile of v1, /device:TPU:0, one launch (start us, length us, event | category | flops | bytes accessed | tf_op | source)
XLA Modules:
  0.0 112.1 jit_solution(16638976192132530951)
XLA Ops:
  0.6 106.9 %step.1 = (f32[1024,512]{1,0:T(8,128)}, f32[1024,512]{1,0:T(8,128)}) custom-call(f32[1024,512]{1,0:T(8,128)} %panel_ref.1, f32[1024,512]{1,0:T(8,128)} %trail_ref.1), custom_call_target="tpu_custom_call" | custom-call | tf_op jit(solution)/shard_map/step/pallas_call | solution.py:683
  107.5 0.0 copy-start
  107.6 3.2 %copy.6 = f32[1024,512]{1,0:T(8,128)} copy(f32[1024,512]{1,0:T(8,128)} %get-tuple-element.4) | data formatting | bytes 4194304
  110.8 0.0 copy-done
  110.8 1.3 %copy.7 = f32[1024,512]{1,0:T(8,128)} copy(f32[1024,512]{1,0:T(8,128)S(1)} %copy-done) | data formatting | bytes 4194304
Async XLA Ops:
  107.5 3.2 %copy-start = (f32[1024,512]{1,0:T(8,128)S(1)}, f32[1024,512]{1,0:T(8,128)}, u32[]{:S(2)}) copy-start(f32[1024,512]{1,0:T(8,128)} %get-tuple-element.5) | copy-start | bytes 6291460

commit v2 on v1

--- a/solution.py
+++ b/solution.py
@@ -453,7 +453,7 @@
         wait(z_third())
         start(z_fourth())
 
-    def hook3():
+    def mid3():
         wait(gather_a(zs, az0, az1, AZA))
         start(gather_b(az0, az1, AZB))
 
@@ -498,12 +498,8 @@
             pan_third(1 - k, 0).wait_recv()
             pan_third(k, 1).wait_recv()
 
-    def hook7():
+    def hook8():
         block_arrive(qc, QQ, 0)
-
-    def hook8():
-        wait(block_third(qc, QQ))
-        wait(gather_b(az0, az1, AZB))
 
         @pl.when(giver)
         def _():
@@ -533,7 +529,7 @@
 
 
     mids = {0: mid0, 1: mid1, 2: mid2}
-    hooks = {0: hook0, 1: hook1, 2: hook2, 3: hook3, 4: hook4, 6: hook6, 7: hook7, 8: hook8}
+    hooks = {0: hook0, 1: hook1, 2: hook2, 3: mid3, 4: hook4, 6: hook6, 8: hook8}
     r_i = lax.broadcasted_iota(jnp.int32, (B, B), 0)
     c_i = lax.broadcasted_iota(jnp.int32, (B, B), 1)
     eye = (r_i == c_i).astype(jnp.float32)
@@ -573,14 +569,14 @@
             r_ref[a:b, a:b] = rpp
             rit_ref[a:b, a:b] = linv
             if p:
-                rit_ref[a:b, :a] = dot(linv, rit_ref[a:b, :a])
+                rit_ref[a:b, :a] = dot3(linv, rit_ref[a:b, :a])
             s_ref[a:b, a:b] += rpp
             if b < NB:
                 rrow = dot(linv, x_ref[a:b, b:])
                 r_ref[a:b, b:] = rrow
                 s_ref[a:b, b:] += rrow
                 x_ref[b:, b:] -= dot_t(rrow, rrow)
-                rit_ref[b:, :b] -= dot_t(rrow, rit_ref[a:b, :b])
+                rit_ref[b:, :b] -= dot3(rrow.T, rit_ref[a:b, :b])
         if p > 0:
             a, b = a - B, b - B
             lui = e_ref[1, :, B:]
@@ -589,14 +585,14 @@
             lui_ref[a:b, a:b] = lui
             mi_ref[a:b, a:b] = mi
             if a:
-                lui_ref[a:b, :a] = dot(lui, lui_ref[a:b, :a])
-                mi_ref[:a, a:b] = dot(mi_ref[:a, a:b], mi)
+                lui_ref[a:b, :a] = dot3(lui, lui_ref[a:b, :a])
+                mi_ref[:a, a:b] = dot3(mi_ref[:a, a:b], mi)
             if b < NB:
                 mrow = dot(lui, s_ref[a:b, b:])
                 lucol = dot(s_ref[b:, a:b], mi)
                 s_ref[b:, b:] -= dot(lucol, mrow)
-                lui_ref[b:, :b] -= dot(lucol, lui_ref[a:b, :b])
-                mi_ref[:b, b:] -= dot(mi_ref[:b, a:b], mrow)
+                lui_ref[b:, :b] -= dot3(lucol, lui_ref[a:b, :b])
+                mi_ref[:b, b:] -= dot3(mi_ref[:b, a:b], mrow)
 
     def phase(ph, carry):
         for p in range(NPH + 1):
@@ -616,20 +612,21 @@
     k2t[...] = dot3(lui_ref[...], rit_ref[...])
     k2 = split(k2t[...])
     lui = split(lui_ref[...])
+    def shifted(q):
+        block = panel_ref[256 * q : 256 * (q + 1), :]
+        if q < 2:
+            block = block + jnp.where(r == 0, r_ref[256 * q : 256 * (q + 1), :], 0.0)
+        return block
+
+    for q in range(4):
+        wr[256 * q : 256 * (q + 1), :] = dot3(shifted(q), k2, NT)
+    wait(gather_b(az0, az1, AZB))
     for az, ax, h in ((az0, ax0, 0), (az1, ax1, 1)):
         val = dot3(az[...].reshape(NB, NB), k2, NT) + dot3(ax[...].reshape(NB, NB), lui, NT)
         for n in range(16):
             j = 4 * (n % 4) + n // 4 if h == 0 else n
             img[64 * j + 32 * h : 64 * j + 32 * h + 32, :] = val[32 * n : 32 * n + 32, :]
 
-    def shifted(q):
-        block = panel_ref[256 * q : 256 * (q + 1), :]
-        if q < 2:
-            block = block + jnp.where(r == 0, r_ref[256 * q : 256 * (q + 1), :], 0.0)
-        return block
-
-    for q in range(4):
-        wr[256 * q : 256 * (q + 1), :] = dot3(shifted(q), k2, NT)
     curv.fill(lambda i: dot3(wr[:, i * T : (i + 1) * T].T, img[:, i * T :]))
     start(curv.first())
     mi = split(mi_ref[...])
@@ -646,6 +643,7 @@
     wait(curv.second())
     curv.add_ring()
     start(curv.third())
+    wait(block_third(qc, QQ))
     yct[...] = dot3(k2, zc[...].reshape(NB, NB), NT) + dot3(lui, qc[...].reshape(NB, NB))
     wait(curv.third())
     start(curv.fourth())

time: 113 us -> 113 us (level); the launches traced: 112 us -> 111 us
    pallas_call x1, Pallas kernels: 107 us -> 106 us  [on_device(): pl.pallas_call(step_kernel, out_shape=[jax.ShapeDtypeStruct((1024, NB), f...]
where the time goes in v2:
time: 113 us; the launch traced here: 111 us
  Pallas kernels  106 us (94%)
  local copies, waits for them, and re-layouts  4.55 us (4%)
    pallas_call x1, Pallas kernels, on_device(): pl.pallas_call(step_kernel, out_shape=[jax.ShapeDtypeStruct((1024, NB), f...  106 us
    unnamed x4, local copies, waits for them, and re-layouts  4.55 us

profile of v2, /device:TPU:0, one launch (start us, length us, event | category | flops | bytes accessed | tf_op | source)
XLA Modules:
  0.0 110.8 jit_solution(15996664784157393383)
XLA Ops:
  0.6 105.6 %step.1 = (f32[1024,512]{1,0:T(8,128)}, f32[1024,512]{1,0:T(8,128)}) custom-call(f32[1024,512]{1,0:T(8,128)} %panel_ref.1, f32[1024,512]{1,0:T(8,128)} %trail_ref.1), custom_call_target="tpu_custom_call" | custom-call | tf_op jit(solution)/shard_map/step/pallas_call | solution.py:681
  106.2 0.0 copy-start
  106.2 3.2 %copy.6 = f32[1024,512]{1,0:T(8,128)} copy(f32[1024,512]{1,0:T(8,128)} %get-tuple-element.4) | data formatting | bytes 4194304
  109.5 0.0 copy-done
  109.5 1.3 %copy.7 = f32[1024,512]{1,0:T(8,128)} copy(f32[1024,512]{1,0:T(8,128)S(1)} %copy-done) | data formatting | bytes 4194304
Async XLA Ops:
  106.2 3.2 %copy-start = (f32[1024,512]{1,0:T(8,128)S(1)}, f32[1024,512]{1,0:T(8,128)}, u32[]{:S(2)}) copy-start(f32[1024,512]{1,0:T(8,128)} %get-tuple-element.5) | copy-start | bytes 6291460
